TPU v7x, 32 devices: a whole 2x2x4 slice. The times are simulated.
32 devices in a mesh: video: 2 (over x), frame: 4 (over z), head: 4 (over y, core).
Axes of the slice: x: 2, y: 2, z: 4, core: 2. Of those that a mesh axis runs over, the one named last changes fastest.
Arguments:
- latents: bfloat16 [2048, 2560], P(('video', 'frame', 'head')), parts along dimension 0, may hold values from -24 to 24
- weights: bfloat16 [2560, 3, 2560], P(None, None, 'head'), may hold values from -0.125 to 0.125
- key_slots: int32 [16, 4, 4], P('frame'), may hold values from 0 to 3, as said below
- key_count: int32 [16, 4], P('frame'), may hold values from 0 to 4, as said below
Outputs:
- attended: bfloat16 [2048, 2560], P(('video', 'frame'), 'head'), parts along dimension 0
There are 2 independent parts, one for each index of `video`. A program takes and returns all parts, laid end to end along the dimension named above; an argument that names none is the same for every part. Nothing has to cross between parts.
Inputs may be any that keep to these rules, and one draw needn't show every extreme that they name: key_slots[a, b, :] is a permutation of the local block numbers of a slab. key_count[a, b] is 4 when query block a lies in slab b; otherwise it is at most max(1, 4 // p), where p is the largest power of two not above the distance between a's slab and b.
All inputs are finite; a program needn't handle non-finite values.
Results may differ from a plain program's by a relative error of at most 0.012.
The roundings to bfloat16 on the way count: a program that leaves them out, or rounds other values in their place, can miss the bound.
Values may be sent and summed in bfloat16 or wider, within the bound.
A program may use at most 128 MiB of HBM per device.

v0:
```python
import jax
import jax.numpy as jnp
from jax import lax
from jax.sharding import PartitionSpec as P

HD = 128
masked_score = -1e30


def on_device(latents, weights, key_slots, key_count):
    width_in = weights.shape[0]
    local_width = weights.shape[2]
    w_joined = weights.reshape(width_in, 3 * local_width)
    joined = jnp.dot(
        lax.all_gather(latents, "head", axis=0, tiled=True),
        w_joined,
        preferred_element_type=jnp.float32,
    ).astype(jnp.bfloat16)
    slab_len = joined.shape[0]
    head_count = local_width // HD
    query_heads = joined[:, :local_width].reshape(slab_len, head_count, HD)
    keys_here = joined[:, local_width : 2 * local_width]
    values_here = joined[:, 2 * local_width :]
    score_scale = HD ** (-0.5)
    blocks_here = key_slots.shape[0]
    slab_total = key_slots.shape[1]
    per_slab = key_slots.shape[2]
    block_rows = slab_len // blocks_here
    all_blocks = slab_total * per_slab
    block_ids = jnp.arange(per_slab, dtype=jnp.int32)
    listed = jnp.any(
        (key_slots[:, :, :, None] == block_ids[None, None, None, :])
        & (block_ids[None, None, :, None] < key_count[:, :, None, None]),
        axis=2,
    )
    allowed = listed.reshape(blocks_here, all_blocks).astype(jnp.float32)

    def compute(state, key_part, value_part, visible):
        row_count = key_part.shape[0]
        top_score, denominator, numerator = state
        scores = (
            jnp.einsum(
                "qhd,khd->hqk",
                query_heads,
                key_part.reshape(row_count, head_count, HD),
                preferred_element_type=jnp.float32,
            )
            * score_scale
        )
        scores = jnp.where(visible[None], scores, masked_score)
        new_top = jnp.maximum(top_score, jnp.max(scores, axis=-1))
        rescale = jnp.exp(top_score - new_top)
        shares = jnp.exp(scores - new_top[:, :, None])
        denominator = denominator * rescale + jnp.sum(shares, axis=-1)
        update = jnp.einsum(
            "hqk,khd->qhd",
            shares.astype(jnp.bfloat16),
            value_part.reshape(row_count, head_count, HD),
            preferred_element_type=jnp.float32,
        )
        numerator = numerator * jnp.transpose(rescale)[:, :, None] + update
        return (new_top, denominator, numerator)

    def attend_rows(running, key_part, value_part, first_row):
        row_count = key_part.shape[0]
        row_blocks = (first_row + jnp.arange(row_count, dtype=jnp.int32)) // block_rows
        onehot = (jnp.arange(all_blocks, dtype=jnp.int32)[:, None] == row_blocks[None, :]).astype(
            jnp.float32
        )
        listed_here = jnp.dot(allowed, onehot) > 0.5
        visible = jnp.broadcast_to(
            listed_here[:, None, :], (blocks_here, block_rows, row_count)
        ).reshape(slab_len, row_count)
        return compute(running, key_part, value_part, visible)

    initial = (
        jnp.full((head_count, slab_len), masked_score, jnp.float32),
        jnp.zeros((head_count, slab_len), jnp.float32),
        jnp.zeros((slab_len, head_count, HD), jnp.float32),
    )
    key_part = lax.all_gather(keys_here, "frame", axis=0, tiled=True)
    value_part = lax.all_gather(values_here, "frame", axis=0, tiled=True)
    row_count = key_part.shape[0]
    step_rows = 512

    def one_block(position, state):
        key_block = lax.dynamic_slice_in_dim(key_part, position * step_rows, step_rows, 0)
        value_block = lax.dynamic_slice_in_dim(value_part, position * step_rows, step_rows, 0)
        return attend_rows(state, key_block, value_block, position * step_rows)

    running = lax.fori_loop(0, row_count // step_rows, one_block, initial)
    top_score, denominator, numerator = running
    mixed = numerator / jnp.transpose(denominator)[:, :, None]
    return mixed.reshape(slab_len, local_width).astype(jnp.bfloat16)


def solution(mesh):
    return jax.shard_map(
        on_device,
        mesh=mesh,
        in_specs=(
            P(("video", "frame", "head"), None),
            P(None, None, "head"),
            P("frame", None, None),
            P("frame", None),
        ),
        out_specs=P(("video", "frame"), "head"),
        check_vma=False,
    )
```

profile of v0, /device:TPU:0, one launch (start us, length us, event | category | flops | bytes accessed | tf_op | source)
XLA Modules:
  0.0 130.2 jit_solution(18211134643761131619)
XLA Ops:
  6.5 0.7 all-gather.4.cloned.1.call-update
  7.3 13.8 %copy.22 = bf16[2560,3,640]{0,2,1:T(8,128)(2,1)} copy(bf16[2560,3,640]{2,0,1:T(8,128)(2,1)} %param.7) | data formatting | bytes 19660800 | tf_op args[1]
  21.1 8.7 %all-gather.4.cloned.1.call-done = bf16[256,2560]{1,0:T(8,128)(2,1)} async-done(((bf16[64,2560]{1,0:T(8,128)(2,1)}), bf16[256,2560]{1,0:T(8,128)(2,1)}) %all-gather.4.cloned.1.call-update) | async-done | bytes 1310736 | tf_op jit(solution)/shard_map/all_gather | solution.py:15
  29.8 7.1 %convolution_convert_fusion = bf16[256,1920]{1,0:T(8,128)(2,1)S(1)} fusion(bf16[256,2560]{1,0:T(8,128)(2,1)} %all-gather.4.cloned.1.call-done, bf16[2560,1920]{0,1:T(8,128)(2,1)} %bitcast.63), kind=kOutput, calls=%fused_computation.35 | convolution fusion | flops 2517073920 | bytes 12124160 | tf_op jit(solution)/shard_map/dot_general | solution.py:14
  37.0 0.9 fusion.26
  38.0 0.7 all-gather.8.cloned.1.call-update
  39.2 0.9 copy.25
  40.1 30.7 %all-gather.6.cloned.1.call-done = bf16[1024,640]{1,0:T(8,128)(2,1)} async-done(((bf16[256,640]{1,0:T(8,128)(2,1)}), bf16[1024,640]{1,0:T(8,128)(2,1)}) %all-gather.6.cloned.1.call-update) | async-done | bytes 1310736 | tf_op jit(solution)/shard_map/all_gather | solution.py:81
  70.8 33.3 %all-gather.8.cloned.1.call-done = bf16[1024,640]{1,0:T(8,128)(2,1)} async-done(((bf16[256,640]{1,0:T(8,128)(2,1)}), bf16[1024,640]{1,0:T(8,128)(2,1)}) %all-gather.8.cloned.1.call-update) | async-done | bytes 1310736 | tf_op jit(solution)/shard_map/all_gather | solution.py:82
  104.1 17.6 %while.20 = (s32[]{:T(128)}, f32[5,256]{1,0:T(8,128)S(1)}, f32[5,256]{1,0:T(8,128)S(1)}, f32[256,5,128]{0,2,1:T(8,128)}, bf16[4,16]{1,0:T(4,128)(2,1)S(1)}, /*in...) while((s32[]{:T(128)}, f32[5,256]{1,0:T(8,128)S(1)}, ...), condition=%wide.region_4.5_spmd.clone, body=%wide.region_1.4_spmd.clone.sunk | while | flops 343336448 | bytes 16933176 | solution.py:91
  104.1 2.2 %constant_dynamic-slice_fusion.3 = (bf16[512,640]{1,0:T(8,128)(2,1)}, bf16[512,640]{1,0:T(8,128)(2,1)S(1)}) fusion(bf16[1024,640]{1,0:T(8,128)(2,1)} %get-tuple-element.375, s32[]{:T(128)S(6)} %select_n.63, bf16[1024,640]{1,0:T(8,128)(2,1)} %get-tuple-element.373), kind=kLoop, calls=%fused_computation.31.clone.1 | loop fusion | bytes 2621444 | tf_op jit(solution)/shard_map/while/body/eval_jaxpr/dynamic_slice | solution.py:88
  106.8 0.3 copy.35
  107.0 1.6 %fusion.50 = (f32[5,256]{1,0:T(8,128)S(1)}, f32[5,512,256]{2,1,0:T(8,128)S(1)}) fusion(pred[256,512]{0,1:T(8,128)(4,1)S(1)} %copy.35, bf16[512,5,128]{0,2,1:T(8,128)(2,1)S(1)} %bitcast.60, bf16[256,5,128]{2,0,1:T(8,128)(2,1)} %get-tuple-element.374), kind=kOutput, calls=%fused_computation.4.clone.1 | convolution fusion | flops 169736960 | bytes 3740672 | tf_op jit(solution)/shard_map/while/body/eval_jaxpr/qhd,khd->hqk/dot_general | solution.py:42
  108.7 1.3 %copy.37 = bf16[512,640]{0,1:T(8,128)(2,1)S(1)} copy(bf16[512,640]{1,0:T(8,128)(2,1)} %get-tuple-element.342) | data formatting | bytes 1310720 | tf_op jit(solution)/shard_map/while/body/eval_jaxpr/dynamic_slice | solution.py:88
  110.0 1.7 %fusion.54 = f32[256,5,128]{0,2,1:T(8,128)} fusion(bf16[512,5,128]{0,2,1:T(8,128)(2,1)S(1)} %bitcast.61, f32[5,512,256]{2,1,0:T(8,128)S(1)} %get-tuple-element.341, f32[5,256]{1,0:T(8,128)S(1)} %get-tuple-element.369, pred[256,512]{0,1:T(8,128)(4,1)S(1)} %copy.35, f32[256,5,128]{0,2,1:T(8,128)} %get-tuple-element.359, ...), kind=kOutput, calls=%fused_computation.11.clone.1 | convolution fusion | flops 170885120 | bytes 4728833 | tf_op jit(solution)/shard_map/while/body/eval_jaxpr/hqk,khd->qhd/dot_general | solution.py:55
  111.7 0.6 fusion.52
  112.3 2.2 %constant_dynamic-slice_fusion.3 = (bf16[512,640]{1,0:T(8,128)(2,1)}, bf16[512,640]{1,0:T(8,128)(2,1)S(1)}) fusion(bf16[1024,640]{1,0:T(8,128)(2,1)} %get-tuple-element.375, s32[]{:T(128)S(6)} %select_n.63, bf16[1024,640]{1,0:T(8,128)(2,1)} %get-tuple-element.373), kind=kLoop, calls=%fused_computation.31.clone.1 | loop fusion | bytes 2621444 | tf_op jit(solution)/shard_map/while/body/eval_jaxpr/dynamic_slice | solution.py:88
  115.0 0.3 copy.35
  115.3 1.6 %fusion.50 = (f32[5,256]{1,0:T(8,128)S(1)}, f32[5,512,256]{2,1,0:T(8,128)S(1)}) fusion(pred[256,512]{0,1:T(8,128)(4,1)S(1)} %copy.35, bf16[512,5,128]{0,2,1:T(8,128)(2,1)S(1)} %bitcast.60, bf16[256,5,128]{2,0,1:T(8,128)(2,1)} %get-tuple-element.374), kind=kOutput, calls=%fused_computation.4.clone.1 | convolution fusion | flops 169736960 | bytes 3740672 | tf_op jit(solution)/shard_map/while/body/eval_jaxpr/qhd,khd->hqk/dot_general | solution.py:42
  116.9 1.3 %copy.37 = bf16[512,640]{0,1:T(8,128)(2,1)S(1)} copy(bf16[512,640]{1,0:T(8,128)(2,1)} %get-tuple-element.342) | data formatting | bytes 1310720 | tf_op jit(solution)/shard_map/while/body/eval_jaxpr/dynamic_slice | solution.py:88
  118.3 2.8 %fusion.54 = f32[256,5,128]{0,2,1:T(8,128)} fusion(bf16[512,5,128]{0,2,1:T(8,128)(2,1)S(1)} %bitcast.61, f32[5,512,256]{2,1,0:T(8,128)S(1)} %get-tuple-element.341, f32[5,256]{1,0:T(8,128)S(1)} %get-tuple-element.369, pred[256,512]{0,1:T(8,128)(4,1)S(1)} %copy.35, f32[256,5,128]{0,2,1:T(8,128)} %get-tuple-element.359, ...), kind=kOutput, calls=%fused_computation.11.clone.1 | convolution fusion | flops 170885120 | bytes 4728833 | tf_op jit(solution)/shard_map/while/body/eval_jaxpr/hqk,khd->qhd/dot_general | solution.py:55
  121.0 0.6 fusion.52
  121.6 1.1 divide_convert_fusion
  122.8 0.9 copy.27
  (30 shorter events, 1.5 us)
Async XLA Ops:
  6.5 23.3 %all-gather.4.cloned.1.call-start = ((), (), s32[]{:S(2)}) async-start(), calls=%async_computation | async-start | bytes 1638400 | tf_op jit(solution)/shard_map/all_gather | solution.py:15
  7.3 63.5 %all-gather.6.cloned.1.call-start = ((), (), s32[]{:S(2)}) async-start(), calls=%async_computation.1 | async-start | bytes 1638400 | tf_op jit(solution)/shard_map/all_gather | solution.py:81
  36.9 1.7 %copy-start.1 = (s32[4,4]{1,0:T(4,128)S(1)}, s32[4,4]{1,0:T(4,128)}, u32[]{:S(2)}) copy-start(s32[4,4]{1,0:T(4,128)} %param.9) | copy-start | bytes 196
  37.0 1.8 %copy-start = (s32[4,4,4]{2,1,0:T(4,128)S(1)}, s32[4,4,4]{2,1,0:T(4,128)}, u32[]{:S(2)}) copy-start(s32[4,4,4]{2,1,0:T(4,128)} %param.8) | copy-start | bytes 772
  37.9 66.2 %all-gather.8.cloned.1.call-start = ((), (), s32[]{:S(2)}) async-start(), calls=%async_computation.2 | async-start | bytes 1638400 | tf_op jit(solution)/shard_map/all_gather | solution.py:82
Sparse Core Ops, SparseCore 0:
  8.9 20.8 all-gather.3
  38.0 32.6 all-gather.5
  72.3 31.6 all-gather.7
where the time goes:
time: 131 us; the launch traced here: 130 us
  waiting for transfers between devices  74.1 us (57%)
  local copies, waits for them, and re-layouts  25.1 us (19%)
  matrix products  15.1 us (12%)
  between operations  13.2 us (10%)
  other arithmetic  2.52 us (2%)
    all_gather x1, waiting for transfers between devices, on_device(): value_part = lax.all_gather(values_here, 'frame', axis=0, tiled=True)  33.3 us
    all_gather x1, waiting for transfers between devices, on_device(): key_part = lax.all_gather(keys_here, 'frame', axis=0, tiled=True)  30.7 us
    unnamed x6, local copies, waits for them, and re-layouts  14.7 us
    all_gather x1, waiting for transfers between devices, on_device(): lax.all_gather(latents, 'head', axis=0, tiled=True)  8.7 us
    dynamic_slice x4, local copies, waits for them, and re-layouts, one_block(): lax.dynamic_slice_in_dim(value_part, position * step_rows, step_rows, 0)  7.14 us
    dot_general x1, matrix products, on_device(): jnp.dot(lax.all_gather(latents, 'head', axis=0, tiled=True), w_joined, pr...  7.09 us
    dot_general x2, matrix products, compute(): jnp.einsum('hqk,khd->qhd', shares.astype(jnp.bfloat16), value_part.reshap...  4.46 us
    dot_general x2, matrix products, compute(): jnp.einsum('qhd,khd->hqk', query_heads, key_part.reshape(row_count, head_...  3.27 us
  transfers between devices with their start and end apart: 3, of which 3 were waited for; matrix products, arithmetic and copies ran while one was open for 12% of the time, Pallas kernels for 0%

commit v1 on v0

--- a/solution.py
+++ b/solution.py
@@ -5,6 +5,26 @@
 
 HD = 128
 masked_score = -1e30
+
+
+def _mix_pairs_all(base_x):
+    part_now, current_value, vec_out = (
+        jax.lax.axis_size("frame"),
+        jax.lax.axis_index("frame"),
+        base_x.shape[0],
+    )
+    leaves = [at * part_now if ii == 0 else at for ii, at in enumerate(base_x.shape)]
+    fresh = lax.dynamic_update_slice_in_dim(
+        jnp.zeros(leaves, base_x.dtype), base_x, current_value * vec_out, axis=0
+    )
+    for src_i in range(1, part_now):
+        base_x = jax.lax.ppermute(
+            base_x, axis_name="frame", perm=[(ii, (ii + 1) % part_now) for ii in range(part_now)]
+        )
+        fresh = lax.dynamic_update_slice_in_dim(
+            fresh, base_x, (current_value - src_i) % part_now * vec_out, axis=0
+        )
+    return fresh
 
 
 def on_device(latents, weights, key_slots, key_count):
@@ -79,7 +99,7 @@
         jnp.zeros((slab_len, head_count, HD), jnp.float32),
     )
     key_part = lax.all_gather(keys_here, "frame", axis=0, tiled=True)
-    value_part = lax.all_gather(values_here, "frame", axis=0, tiled=True)
+    value_part = _mix_pairs_all(values_here)
     row_count = key_part.shape[0]
     step_rows = 512
 

time: 131 us -> 111 us (0.85)
  waiting for transfers between devices: 74.1 us -> 44.5 us
  starting transfers between devices: 0.08 us -> 6.69 us
  local copies, waits for them, and re-layouts: 25.1 us -> 27.5 us
    ppermute x0 -> x3, waiting for transfers between devices: none -> 35.1 us  [_mix_pairs_all(): jax.lax.ppermute(base_x, axis_name='frame', perm=[(ii, (ii + 1) % part_no...]
    all_gather x1 -> x0, waiting for transfers between devices: 33.3 us -> none  [on_device(): value_part = lax.all_gather(values_here, 'frame', axis=0, tiled=True)]
    all_gather x1, waiting for transfers between devices: 30.7 us -> 0.01 us  [on_device(): key_part = lax.all_gather(keys_here, 'frame', axis=0, tiled=True)]
    ppermute x0 -> x3, starting transfers between devices: none -> 6.65 us  [_mix_pairs_all(): jax.lax.ppermute(base_x, axis_name='frame', perm=[(ii, (ii + 1) % part_no...]
    dynamic_slice x4 -> x2, local copies, waits for them, and re-layouts: 7.14 us -> 2.28 us  [one_block(): lax.dynamic_slice_in_dim(value_part, position * step_rows, step_rows, 0)]
    dynamic_update_slice x0 -> x4, local copies, waits for them, and re-layouts: none -> 3.18 us  [the longest x3 2.38 us: _mix_pairs_all(): lax.dynamic_update_slice_in_dim(fresh, base_x, (current_value - src_i) %...]
    dynamic_slice x2 -> x4, local copies, waits for them, and re-layouts: 0.5 us -> 2.8 us  [one_block(): lax.dynamic_slice_in_dim(key_part, position * step_rows, step_rows, 0)]
  transfers between devices with their start and end apart: 3 -> 5, of which waited for: 3 -> 4; matrix products, arithmetic and copies ran while one was open for 12% -> 18% of each run, Pallas kernels for 0% -> 0%
where the time goes in v1:
time: 111 us; the launch traced here: 110 us
  waiting for transfers between devices  44.5 us (40%)
  local copies, waits for them, and re-layouts  27.5 us (25%)
  matrix products  15.1 us (14%)
  between operations  13.5 us (12%)
  starting transfers between devices  6.69 us (6%)
  other arithmetic  2.52 us (2%)
    ppermute x3, waiting for transfers between devices, _mix_pairs_all(): jax.lax.ppermute(base_x, axis_name='frame', perm=[(ii, (ii + 1) % part_no...  35.1 us
    unnamed x6, local copies, waits for them, and re-layouts  14.8 us
    all_gather x1, waiting for transfers between devices, on_device(): lax.all_gather(latents, 'head', axis=0, tiled=True)  8.69 us
    dot_general x1, matrix products, on_device(): jnp.dot(lax.all_gather(latents, 'head', axis=0, tiled=True), w_joined, pr...  7.12 us
    ppermute x3, starting transfers between devices, _mix_pairs_all(): jax.lax.ppermute(base_x, axis_name='frame', perm=[(ii, (ii + 1) % part_no...  6.65 us
    dot_general x2, matrix products, compute(): jnp.einsum('hqk,khd->qhd', shares.astype(jnp.bfloat16), value_part.reshap...  4.47 us
    dot_general x2, matrix products, compute(): jnp.einsum('qhd,khd->hqk', query_heads, key_part.reshape(row_count, head_...  3.26 us
    dynamic_slice x4, local copies, waits for them, and re-layouts, one_block(): lax.dynamic_slice_in_dim(key_part, position * step_rows, step_rows, 0)  2.8 us
  transfers between devices with their start and end apart: 5, of which 4 were waited for; matrix products, arithmetic and copies ran while one was open for 18% of the time, Pallas kernels for 0%

profile of v1, /device:TPU:0, one launch (start us, length us, event | category | flops | bytes accessed | tf_op | source)
XLA Modules:
  0.0 110.0 jit_solution(1039178783722528607)
XLA Ops:
  7.3 13.9 %copy.28 = bf16[2560,3,640]{0,2,1:T(8,128)(2,1)} copy(bf16[2560,3,640]{2,0,1:T(8,128)(2,1)} %param.7) | data formatting | bytes 19660800 | tf_op args[1]
  21.2 8.7 %all-gather.3.cloned.1.call-done = bf16[256,2560]{1,0:T(8,128)(2,1)} async-done(((bf16[64,2560]{1,0:T(8,128)(2,1)}), bf16[256,2560]{1,0:T(8,128)(2,1)}) %all-gather.3.cloned.1.call-update) | async-done | bytes 1310736 | tf_op jit(solution)/shard_map/all_gather | solution.py:35
  29.8 7.1 %convolution_convert_fusion = bf16[256,1920]{1,0:T(8,128)(2,1)S(1)} fusion(bf16[256,2560]{1,0:T(8,128)(2,1)} %all-gather.3.cloned.1.call-done, bf16[2560,1920]{0,1:T(8,128)(2,1)} %bitcast.63), kind=kOutput, calls=%fused_computation.35 | convolution fusion | flops 2517073920 | bytes 12124160 | tf_op jit(solution)/shard_map/dot_general | solution.py:34
  37.0 0.8 fusion.26
  37.8 1.5 %collective-permute-start = (bf16[256,640]{1,0:T(8,128)(2,1)S(1)}, bf16[256,640]{1,0:T(8,128)(2,1)S(1)}, u32[]{:S(2)}, u32[]{:S(2)}) collective-permute-start(bf16[256,640]{1,0:T(8,128)(2,1)S(1)} %get-tuple-element.278), channel_id=1, source_target_pairs={{0,4},{4,8},{8,12},{12,0},{1,5},{5,9},{9,13},{13,1},{2,6},{6,10},{... | collective-permute-start | bytes 983048 | tf_op jit(solution)/shard_map/ppermute | solution.py:21
  39.3 10.3 %collective-permute-done = bf16[256,640]{1,0:T(8,128)(2,1)S(1)} collective-permute-done((bf16[256,640]{1,0:T(8,128)(2,1)S(1)}, bf16[256,640]{1,0:T(8,128)(2,1)S(1)}, u32[]{:S(2)}, u32[]{:S(2)}) %collective-permute-start) | collective-permute-done | bytes 327712 | tf_op jit(solution)/shard_map/ppermute | solution.py:21
  51.1 0.9 copy.35
  52.0 16.5 %collective-permute-done.1 = bf16[256,640]{1,0:T(8,128)(2,1)S(1)} collective-permute-done((bf16[256,640]{1,0:T(8,128)(2,1)S(1)}, bf16[256,640]{1,0:T(8,128)(2,1)S(1)}, u32[]{:S(2)}, u32[]{:S(2)}) %collective-permute-start.1) | collective-permute-done | bytes 327712 | tf_op jit(solution)/shard_map/ppermute | solution.py:21
  68.4 4.3 %collective-permute-start.2 = (bf16[256,640]{1,0:T(8,128)(2,1)S(1)}, bf16[256,640]{1,0:T(8,128)(2,1)S(1)}, u32[]{:S(2)}, u32[]{:S(2)}) collective-permute-start(bf16[256,640]{1,0:T(8,128)(2,1)S(1)} %collective-permute-done.1), channel_id=1, source_target_pairs={{0,4},{4,8},{8,12},{12,0},{1,5},{5,9},{9,13},{13,1},{2,6},{6,10},{... | collective-permute-start | bytes 983048 | tf_op jit(solution)/shard_map/ppermute | solution.py:21
  72.8 1.2 %broadcast_in_dim.88 = bf16[1024,640]{0,1:T(8,128)(2,1)} broadcast(bf16[]{:T(256)} %constant.161.clone.1), dimensions={} | broadcast | bytes 1310722 | tf_op jit(solution)/shard_map/broadcast_in_dim | solution.py:18
  74.0 0.8 constant_dynamic-update-slice_fusion.3
  75.0 0.8 constant_dynamic-update-slice_fusion.2
  76.8 8.4 %collective-permute-done.2 = bf16[256,640]{1,0:T(8,128)(2,1)S(1)} collective-permute-done((bf16[256,640]{1,0:T(8,128)(2,1)S(1)}, bf16[256,640]{1,0:T(8,128)(2,1)S(1)}, u32[]{:S(2)}, u32[]{:S(2)}) %collective-permute-start.2) | collective-permute-done | bytes 327712 | tf_op jit(solution)/shard_map/ppermute | solution.py:21
  86.1 15.0 %while.20 = (s32[]{:T(128)}, f32[5,256]{1,0:T(8,128)S(1)}, f32[5,256]{1,0:T(8,128)S(1)}, f32[256,5,128]{0,2,1:T(8,128)}, bf16[4,16]{1,0:T(4,128)(2,1)S(1)}, /*in...) while((s32[]{:T(128)}, f32[5,256]{1,0:T(8,128)S(1)}, ...), condition=%wide.region_4.5_spmd.clone, body=%wide.region_1.4_spmd.clone.sunk | while | flops 343336448 | bytes 15622459 | solution.py:111
  86.1 1.1 %constant_dynamic-slice_fusion.4 = bf16[512,640]{1,0:T(8,128)(2,1)S(1)} fusion(bf16[1024,640]{1,0:T(8,128)(2,1)} %get-tuple-element.367, s32[]{:T(128)S(6)} %select_n.97), kind=kLoop, calls=%fused_computation.32.clone.1 | loop fusion | bytes 1310724 | tf_op jit(solution)/shard_map/while/body/eval_jaxpr/dynamic_slice | solution.py:107
  88.0 1.6 %fusion.50 = (f32[5,256]{1,0:T(8,128)S(1)}, f32[5,512,256]{2,1,0:T(8,128)S(1)}) fusion(pred[256,512]{0,1:T(8,128)(4,1)S(1)} %copy.42, bf16[512,5,128]{0,2,1:T(8,128)(2,1)S(1)} %bitcast.60, bf16[256,5,128]{2,0,1:T(8,128)(2,1)} %get-tuple-element.368), kind=kOutput, calls=%fused_computation.4.clone.1 | convolution fusion | flops 169736960 | bytes 3740672 | tf_op jit(solution)/shard_map/while/body/eval_jaxpr/qhd,khd->hqk/dot_general | solution.py:62
  89.7 1.1 %constant_dynamic-slice_fusion.5 = bf16[512,640]{0,1:T(8,128)(2,1)S(1)} fusion(bf16[1024,640]{0,1:T(8,128)(2,1)} %get-tuple-element.369, s32[]{:T(128)S(6)} %select_n.97), kind=kLoop, calls=%fused_computation.31.clone.1 | loop fusion | bytes 1310724 | tf_op jit(solution)/shard_map/while/body/eval_jaxpr/dynamic_slice | solution.py:108
  90.8 1.7 %fusion.54 = f32[256,5,128]{0,2,1:T(8,128)} fusion(bf16[512,5,128]{0,2,1:T(8,128)(2,1)S(1)} %bitcast.61, f32[5,512,256]{2,1,0:T(8,128)S(1)} %get-tuple-element.336, f32[5,256]{1,0:T(8,128)S(1)} %get-tuple-element.363, pred[256,512]{0,1:T(8,128)(4,1)S(1)} %copy.42, f32[256,5,128]{0,2,1:T(8,128)} %get-tuple-element.353, ...), kind=kOutput, calls=%fused_computation.11.clone.1 | convolution fusion | flops 170885120 | bytes 4728833 | tf_op jit(solution)/shard_map/while/body/eval_jaxpr/hqk,khd->qhd/dot_general | solution.py:75
  93.1 1.1 %constant_dynamic-slice_fusion.4 = bf16[512,640]{1,0:T(8,128)(2,1)S(1)} fusion(bf16[1024,640]{1,0:T(8,128)(2,1)} %get-tuple-element.367, s32[]{:T(128)S(6)} %select_n.97), kind=kLoop, calls=%fused_computation.32.clone.1 | loop fusion | bytes 1310724 | tf_op jit(solution)/shard_map/while/body/eval_jaxpr/dynamic_slice | solution.py:107
  95.0 1.6 %fusion.50 = (f32[5,256]{1,0:T(8,128)S(1)}, f32[5,512,256]{2,1,0:T(8,128)S(1)}) fusion(pred[256,512]{0,1:T(8,128)(4,1)S(1)} %copy.42, bf16[512,5,128]{0,2,1:T(8,128)(2,1)S(1)} %bitcast.60, bf16[256,5,128]{2,0,1:T(8,128)(2,1)} %get-tuple-element.368), kind=kOutput, calls=%fused_computation.4.clone.1 | convolution fusion | flops 169736960 | bytes 3740672 | tf_op jit(solution)/shard_map/while/body/eval_jaxpr/qhd,khd->hqk/dot_general | solution.py:62
  96.6 1.1 %constant_dynamic-slice_fusion.5 = bf16[512,640]{0,1:T(8,128)(2,1)S(1)} fusion(bf16[1024,640]{0,1:T(8,128)(2,1)} %get-tuple-element.369, s32[]{:T(128)S(6)} %select_n.97), kind=kLoop, calls=%fused_computation.31.clone.1 | loop fusion | bytes 1310724 | tf_op jit(solution)/shard_map/while/body/eval_jaxpr/dynamic_slice | solution.py:108
  97.8 2.8 %fusion.54 = f32[256,5,128]{0,2,1:T(8,128)} fusion(bf16[512,5,128]{0,2,1:T(8,128)(2,1)S(1)} %bitcast.61, f32[5,512,256]{2,1,0:T(8,128)S(1)} %get-tuple-element.336, f32[5,256]{1,0:T(8,128)S(1)} %get-tuple-element.363, pred[256,512]{0,1:T(8,128)(4,1)S(1)} %copy.42, f32[256,5,128]{0,2,1:T(8,128)} %get-tuple-element.353, ...), kind=kOutput, calls=%fused_computation.11.clone.1 | convolution fusion | flops 170885120 | bytes 4728833 | tf_op jit(solution)/shard_map/while/body/eval_jaxpr/hqk,khd->qhd/dot_general | solution.py:75
  101.1 1.1 %divide_convert_fusion = bf16[256,5,128]{0,2,1:T(8,128)(2,1)S(1)} fusion(f32[256,5,128]{0,2,1:T(8,128)} %get-tuple-element.205, f32[256,5]{0,1:T(8,128)S(1)} %bitcast.66), kind=kLoop, calls=%fused_computation.36 | loop fusion | flops 327680 | bytes 988160 | tf_op jit(solution)/shard_map/convert_element_type | solution.py:114
  102.3 0.9 copy.36
  (42 shorter events, 6.8 us)
Async XLA Ops:
  6.5 23.3 %all-gather.3.cloned.1.call-start = ((), (), s32[]{:S(2)}) async-start(), calls=%async_computation | async-start | bytes 1638400 | tf_op jit(solution)/shard_map/all_gather | solution.py:35
  7.3 78.9 %all-gather.5.cloned.1.call-start = ((), (), s32[]{:S(2)}) async-start(), calls=%async_computation.1 | async-start | bytes 1638400 | tf_op jit(solution)/shard_map/all_gather | solution.py:101
  29.8 20.6 %copy-start.1 = (s32[4,4]{1,0:T(4,128)S(1)}, s32[4,4]{1,0:T(4,128)}, u32[]{:S(2)}) copy-start(s32[4,4]{1,0:T(4,128)} %param.9) | copy-start | bytes 196
  29.8 20.6 %copy-start = (s32[4,4,4]{2,1,0:T(4,128)S(1)}, s32[4,4,4]{2,1,0:T(4,128)}, u32[]{:S(2)}) copy-start(s32[4,4,4]{2,1,0:T(4,128)} %param.8) | copy-start | bytes 772
  37.8 11.8 %collective-permute-start = (bf16[256,640]{1,0:T(8,128)(2,1)S(1)}, bf16[256,640]{1,0:T(8,128)(2,1)S(1)}, u32[]{:S(2)}, u32[]{:S(2)}) collective-permute-start(bf16[256,640]{1,0:T(8,128)(2,1)S(1)} %get-tuple-element.278), channel_id=1, source_target_pairs={{0,4},{4,8},{8,12},{12,0},{1,5},{5,9},{9,13},{13,1},{2,6},{6,10},{... | collective-permute-start | bytes 983048 | tf_op jit(solution)/shard_map/ppermute | solution.py:21
  49.6 18.8 %collective-permute-start.1 = (bf16[256,640]{1,0:T(8,128)(2,1)S(1)}, bf16[256,640]{1,0:T(8,128)(2,1)S(1)}, u32[]{:S(2)}, u32[]{:S(2)}) collective-permute-start(bf16[256,640]{1,0:T(8,128)(2,1)S(1)} %collective-permute-done), channel_id=1, source_target_pairs={{0,4},{4,8},{8,12},{12,0},{1,5},{5,9},{9,13},{13,1},{2,6},{6,10},{... | collective-permute-start | bytes 983048 | tf_op jit(solution)/shard_map/ppermute | solution.py:21
  68.4 16.7 %collective-permute-start.2 = (bf16[256,640]{1,0:T(8,128)(2,1)S(1)}, bf16[256,640]{1,0:T(8,128)(2,1)S(1)}, u32[]{:S(2)}, u32[]{:S(2)}) collective-permute-start(bf16[256,640]{1,0:T(8,128)(2,1)S(1)} %collective-permute-done.1), channel_id=1, source_target_pairs={{0,4},{4,8},{8,12},{12,0},{1,5},{5,9},{9,13},{13,1},{2,6},{6,10},{... | collective-permute-start | bytes 983048 | tf_op jit(solution)/shard_map/ppermute | solution.py:21
Sparse Core Ops, SparseCore 0:
  8.9 20.8 all-gather.2
  37.9 41.6 all-gather.4
